TPU v7x, 32 devices: a whole 2x2x4 slice. The times are simulated.
32 devices in a mesh: member: 2 (over y), tile: 4 (over z), nest: 2 (over x), lev: 2 (over core).
Axes of the slice: x: 2, y: 2, z: 4, core: 2. Of those that a mesh axis runs over, the one named last changes fastest.
Arguments:
- parent_field: float32 [10, 2, 256, 512], P('member', None, 'tile', ('nest', 'lev')), parts along dimension 0, may hold values from -6 to 6
- nest_fields: float32 [12, 5, 2, 384, 384], P(('member', 'nest'), None, None, 'tile', 'lev'), parts along dimension 0, may hold values from -6 to 6
- lateral_rate: float32 [5], replicated, may hold values from 0.02 to 0.12
- vertical_rate: float32 [5], replicated, may hold values from 0.02 to 0.12
- centres: int32 [6, 6, 2], P('member'), parts along dimension 0, may hold values from 64 to 448, as said below
- slot_storm: int32 [12], P('member'), parts along dimension 0, may hold values from 0 to 5, each once
Outputs:
- parent_final: float32 [10, 2, 256, 512], P('member', None, 'tile', ('nest', 'lev')), parts along dimension 0
- nest_final: float32 [12, 5, 2, 384, 384], P(('member', 'nest'), None, None, 'tile', 'lev'), parts along dimension 0
There are 2 independent parts, one for each index of `member`. A program takes and returns all parts, laid end to end along the dimension named above; an argument that names none is the same for every part. Nothing has to cross between parts.
Inputs may be any that keep to these rules, and one draw needn't show every extreme that they name: `centres`: from one step to the next the row of a centre changes by 1 to 2 cells in either direction and the column by at most 2 cells; rows stay within 64 to 192 and columns within 64 to 448. `slot_storm`: every storm occupies exactly one nest position.
All inputs are finite; a program needn't handle non-finite values.
Results may differ from a plain program's by a relative error of at most 0.0003.
Values sent between devices are 32-bit elements; how exact they have to be, the bound alone decides.
No kernel may reach another device: no remote copies, remote signals or barrier semaphores. Data moves between devices by JAX's collectives and lax.ppermute only.
A program may use at most 128 MiB of HBM per device.

v0:
```python
import jax
import jax.numpy as jnp
from jax import lax
from jax.sharding import PartitionSpec as P

FP = 128
BWP = 2
MOVE = 2


def extended(cells, sides, width):
    for axis, dim in sides:
        count = lax.axis_size(axis)
        ends = count - 1
        head = lax.slice_in_dim(cells, 0, width, axis=dim)
        tail = lax.slice_in_dim(cells, cells.shape[dim] - width, cells.shape[dim], axis=dim)
        cells = jnp.concatenate(
            [
                lax.ppermute(tail, axis, [(i, (i + 1) % count) for i in range(ends)]),
                cells,
                lax.ppermute(head, axis, [((i + 1) % count, i) for i in range(ends)]),
            ],
            axis=dim,
        )
    return cells


def tendency(padded, lateral_rate, vertical_rate):
    centre = padded[..., 1:-1, 1:-1, 1:-1]
    lateral = (
        padded[..., 1:-1, 2:, 1:-1]
        + padded[..., 1:-1, :-2, 1:-1]
        + padded[..., 1:-1, 1:-1, 2:]
        + padded[..., 1:-1, 1:-1, :-2]
        - 4.0 * centre
    )
    upright = padded[..., 2:, 1:-1, 1:-1] + padded[..., :-2, 1:-1, 1:-1] - 2.0 * centre
    change = (
        lateral_rate[:, None, None, None] * lateral + vertical_rate[:, None, None, None] * upright
    )
    return (centre, change)


def select_rows(picker, table):
    return jnp.sum(picker[:, :, None] * table[None, :, :], axis=1)


def column_block():
    return lax.axis_index("nest") * lax.axis_size("lev") + lax.axis_index("lev")


def extract(parent_now, anchors):
    fields, level_count, parent_rows, parent_cols = parent_now.shape
    padded = jnp.pad(parent_now, ((0, 0), (0, 0), (FP, FP), (FP, FP)))
    rel_rows = anchors[:, 0] - lax.axis_index("tile") * parent_rows + FP
    rel_cols = anchors[:, 1] - column_block() * parent_cols + FP
    zero_index = jnp.zeros((), jnp.int32)

    def single(corner):
        row_at = corner[0]
        col_at = corner[1]
        within = (
            (row_at >= 0)
            & (row_at <= FP + parent_rows)
            & (col_at >= 0)
            & (col_at <= FP + parent_cols)
        )
        row_at = jnp.clip(row_at, 0, FP + parent_rows)
        col_at = jnp.clip(col_at, 0, FP + parent_cols)
        south = lax.dynamic_slice(
            padded, (zero_index, zero_index, row_at, col_at), (fields, level_count, BWP, FP)
        )
        north = lax.dynamic_slice(
            padded,
            (zero_index, zero_index, row_at + FP - BWP, col_at),
            (fields, level_count, BWP, FP),
        )
        west = lax.dynamic_slice(
            padded, (zero_index, zero_index, row_at, col_at), (fields, level_count, FP, BWP)
        )
        east = lax.dynamic_slice(
            padded,
            (zero_index, zero_index, row_at, col_at + FP - BWP),
            (fields, level_count, FP, BWP),
        )
        sides = jnp.stack(
            [south, north, jnp.swapaxes(west, 2, 3), jnp.swapaxes(east, 2, 3)], axis=2
        )
        return jnp.where(within, sides.reshape(fields, level_count, 4 * BWP * FP), 0.0)

    corners = jnp.stack([rel_rows, rel_cols], axis=1)
    return lax.map(single, corners)


def per_device(parent_field, nest_fields, lateral_rate, vertical_rate, centres, slot_storm):
    fields, level_count, parent_rows, parent_cols = parent_field.shape
    slot_count = nest_fields.shape[0]
    strip_rows = nest_fields.shape[3]
    strip_cols = nest_fields.shape[4]
    storm_count = slot_storm.shape[0]
    steps_total = centres.shape[0] - 1
    tile_at = lax.axis_index("tile")
    nest_at = lax.axis_index("nest")
    lev_at = lax.axis_index("lev")
    nest_span = 3 * FP
    reach_rows = 3 * MOVE
    border = 3 * BWP
    zero_index = jnp.zeros((), jnp.int32)
    storm_ids = jnp.arange(storm_count, dtype=jnp.int32)
    pick_all = (slot_storm[:, None] == storm_ids[None, :]).astype(jnp.int32)
    owned = lax.dynamic_slice_in_dim(slot_storm, nest_at * slot_count, slot_count)
    pick_own = (owned[:, None] == storm_ids[None, :]).astype(jnp.int32)
    global_rows = tile_at * strip_rows + jnp.arange(strip_rows, dtype=jnp.int32)
    global_cols = lev_at * strip_cols + jnp.arange(strip_cols, dtype=jnp.int32)
    row_gap = jnp.minimum(global_rows, nest_span - 1 - global_rows)
    col_gap = jnp.minimum(global_cols, nest_span - 1 - global_cols)
    distance = jnp.minimum(row_gap[:, None], col_gap[None, :])
    weight = jnp.maximum(border - distance, 0).astype(jnp.float32) / jnp.float32(border)
    inside = (distance >= 1).astype(jnp.float32)
    coarse_rows = global_rows // 3
    coarse_cols = global_cols // 3
    south_index = jnp.clip(coarse_rows, 0, BWP - 1)
    north_index = jnp.clip(coarse_rows - (FP - BWP), 0, BWP - 1)
    west_index = jnp.clip(coarse_cols, 0, BWP - 1)
    east_index = jnp.clip(coarse_cols - (FP - BWP), 0, BWP - 1)
    near_south = (coarse_rows < BWP)[:, None]
    near_north = (coarse_rows >= FP - BWP)[:, None]
    near_west = (coarse_cols < BWP)[None, :]
    near_east = (coarse_cols >= FP - BWP)[None, :]

    def relocate(single, offset):
        return lax.dynamic_slice(
            single,
            (zero_index, zero_index, reach_rows + offset[0], reach_rows + offset[1]),
            (fields, level_count, strip_rows, strip_cols),
        )

    def across(zone, zone_index):
        picked = jnp.take(zone, zone_index, axis=3)
        return jnp.take(picked, coarse_cols, axis=4)

    def along(zone, zone_index):
        picked = jnp.take(zone, zone_index, axis=3)
        picked = jnp.take(picked, coarse_rows, axis=4)
        return jnp.swapaxes(picked, 3, 4)

    parent_now = parent_field
    nests_now = nest_fields
    for step_index in range(steps_total):
        padded = extended(parent_now, (("tile", 2), (("nest", "lev"), 3)), 1)
        padded = jnp.pad(padded, ((0, 0), (1, 1), (0, 0), (0, 0)))
        centre, change = tendency(padded, lateral_rate, vertical_rate)
        parent_now = centre + change
        later_pos = select_rows(pick_all, centres[step_index + 1])
        anchors = later_pos - FP // 2
        terms = extract(parent_now, anchors)
        totals = lax.psum(terms, ("tile", "nest", "lev"))
        boundary = lax.dynamic_slice_in_dim(totals, nest_at * slot_count, slot_count, 0)
        boundary = boundary.reshape(slot_count, fields, level_count, 4, BWP, FP)
        south_full = across(boundary[:, :, :, 0], south_index)
        north_full = across(boundary[:, :, :, 1], north_index)
        west_full = along(boundary[:, :, :, 2], west_index)
        east_full = along(boundary[:, :, :, 3], east_index)
        sides_full = jnp.where(near_west, west_full, jnp.where(near_east, east_full, 0.0))
        driving = jnp.where(near_south, south_full, jnp.where(near_north, north_full, sides_full))
        own_later = select_rows(pick_own, centres[step_index + 1])
        own_before = select_rows(pick_own, centres[step_index])
        offsets = 3 * (own_later - own_before)
        widened_nests = extended(nests_now, (("tile", 3), ("lev", 4)), reach_rows)
        shifted = jax.vmap(relocate)(widened_nests, offsets)
        source_rows = global_rows[None, :] + offsets[:, 0:1]
        source_cols = global_cols[None, :] + offsets[:, 1:2]
        rows_fine = (source_rows >= 0) & (source_rows < nest_span)
        cols_fine = (source_cols >= 0) & (source_cols < nest_span)
        keep_mask = (rows_fine[:, :, None] & cols_fine[:, None, :])[:, None, None, :, :]
        retained = jnp.where(keep_mask, shifted, driving)
        relaxed = retained + weight * (driving - retained)
        bordered = extended(relaxed, (("tile", 3), ("lev", 4)), 1)
        bordered = jnp.pad(bordered, ((0, 0), (0, 0), (1, 1), (0, 0), (0, 0)))
        centre, change = tendency(bordered, lateral_rate, vertical_rate)
        nests_now = relaxed + inside * change
    return (parent_now, nests_now)


def solution(mesh):
    placed = (
        P("member", None, "tile", ("nest", "lev")),
        P(("member", "nest"), None, None, "tile", "lev"),
        P(),
        P(),
        P("member", None, None),
        P("member"),
    )
    return jax.shard_map(
        per_device,
        mesh=mesh,
        in_specs=placed,
        out_specs=(
            P("member", None, "tile", ("nest", "lev")),
            P(("member", "nest"), None, None, "tile", "lev"),
        ),
        check_vma=False,
    )
```

profile of v0, /device:TPU:0, one launch (start us, length us, event | category | flops | bytes accessed | tf_op | source)
XLA Modules:
  0.0 790.2 jit_solution(10287252542518076452)
XLA Ops:
  65.0 49.2 %while.32 = (s32[]{:T(128)}, f32[6,5,2,1024]{3,2,1,0:T(2,128)S(1)}, s32[6,2]{0,1:T(2,128)S(1)}, f32[5,2,320,384]{2,3,1,0:T(8,128)}, s32[]{:T(128)}, /*index=5*/s...) while((s32[]{:T(128)}, f32[6,5,2,1024]{3,2,1,0:T(2,128)S(1)}, ...), condition=%wide.region_5.6_spmd, body=%wide.region_4.5_spmd.sunk | while | flops 40981 | bytes 450935 | solution.py:92
  136.6 49.5 %while.33 = (s32[]{:T(128)}, f32[6,5,2,1024]{3,2,1,0:T(2,128)S(1)}, s32[6,2]{0,1:T(2,128)S(1)}, f32[5,2,320,384]{2,3,1,0:T(8,128)}, s32[]{:T(128)}, /*index=5*/s...) while((s32[]{:T(128)}, f32[6,5,2,1024]{3,2,1,0:T(2,128)S(1)}, ...), condition=%wide.region_9.14_spmd, body=%wide.region_8.13_spmd.sunk | while | flops 40981 | bytes 450935 | solution.py:92
  186.9 8.2 %pad_maximum_fusion = f32[3,5,2,108,204]{3,2,4,1,0:T(2,128)S(1)} fusion(f32[3,5,2,108,6]{3,2,4,1,0:T(2,128)S(1)} %collective-permute-done.11, f32[3,5,2,6,192]{3,2,4,1,0:T(2,128)} %copy.329, f32[3,5,2,96,192]{3,2,4,1,0:T(2,128)} %copy.328, f32[3,5,2,6,192]{3,2,4,1,0:T(2,128)} %copy.327, f32[3,5,2,108,6]{3,2,4,1,0:T(2,128)} %collective-permute-done.10), kind=kLoop, calls=%fused_computation.46 | loop fusion | flops 2643840 | bytes 5287680 | tf_op jit(solution)/shard_map/concatenate | solution.py:17
  197.5 13.3 %while.34 = (s32[]{:T(128)}, f32[3,5,2,108,204]{3,2,4,1,0:T(2,128)S(1)}, s32[3,5]{1,0:T(4,128)S(1)}, f32[3,5,2,96,192]{3,2,1,0,4:T(2,128)}, s32[]{:T(128)}) while((s32[]{:T(128)}, f32[3,5,2,108,204]{3,2,4,1,0:T(2,128)S(1)}, s32[3,5]{1,0:T(4,128)S(1)}, f32[3,5,2,96,192]{3,2,1,0,4:T(2,128)}, s32[]{:T(128)}) %tuple.212), condition=%wide.while_cond, body=%wide.while_body.sunk | while | flops 2 | bytes 1967757 | solution.py:132
  210.8 70.3 %all-reduce.9.cloned.1.call-done = (f32[6,5,2,1024]{3,2,1,0:T(2,128)}, f32[6,5,2,1024]{3,2,1,0:T(2,128)}) async-done(((f32[6,5,2,1024]{3,2,1,0:T(2,128)}, f32[6,5,2,1024]{3,2,1,0:T(2,128)}), (f32[6,5,2,1024]{3,2,1,0:T(2,128)}, f32[6,5,2,1024]{3,2,1,0:T(2,128)})) %all-reduce.9.cloned.1.call-update) | async-done | bytes 491536 | tf_op jit(solution)/shard_map/psum | solution.py:157
  282.5 12.2 %gather_fusion.14 = f32[192,3,5,2,128]{4,3,2,1,0:T(2,128)S(1)} fusion(f32[3,5,2,2,128]{4,2,3,1,0:T(2,128)S(1)} %bitcast.166, s32[1024]{0:T(1024)S(1)} %pad_clamp_fusion), kind=kCustom, calls=%fused_computation.12.clone | custom fusion | bytes 5899008 | tf_op jit(solution)/shard_map/jit(_take)/gather | solution.py:143
  294.8 11.2 %gather_fusion.6 = f32[192,3,5,2,128]{4,3,2,1,0:T(2,128)} fusion(f32[3,5,2,2,128]{4,2,3,1,0:T(2,128)S(1)} %bitcast.167, s32[1024]{0:T(1024)S(1)} %pad_clamp_fusion), kind=kCustom, calls=%fused_computation.10.clone | custom fusion | bytes 5899008 | tf_op jit(solution)/shard_map/jit(_take)/gather | solution.py:143
  312.8 7.9 %copy.342 = f32[3,5,2,192,128]{3,2,4,1,0:T(2,128)} copy(f32[3,5,2,192,128]{4,2,1,0,3:T(2,128)} %get-tuple-element.471) | data formatting | bytes 5898240 | tf_op jit(solution)/shard_map/jit(_take)/select_n | solution.py:143
  320.7 11.0 %gather_fusion.7 = f32[96,3,5,2,192]{4,3,2,1,0:T(2,128)S(1)} fusion(f32[3,5,2,192,128]{3,2,4,1,0:T(2,128)} %copy.342, s32[1024]{0:T(1024)S(1)} %pad_clamp_fusion.1), kind=kCustom, calls=%fused_computation.13.clone | custom fusion | bytes 4424064 | tf_op jit(solution)/shard_map/jit(_take)/gather | solution.py:144
  337.0 12.2 %gather_fusion.12 = f32[192,3,5,2,128]{4,3,2,1,0:T(2,128)S(1)} fusion(f32[3,5,2,2,128]{4,2,3,1,0:T(2,128)S(1)} %bitcast.169, s32[1024]{0:T(1024)S(1)} %pad_clamp_fusion.2), kind=kCustom, calls=%fused_computation.11.clone | custom fusion | bytes 5899008 | tf_op jit(solution)/shard_map/jit(_take)/gather | solution.py:143
  349.2 10.6 %gather_fusion.4 = f32[192,3,5,2,128]{4,3,2,1,0:T(2,128)} fusion(f32[3,5,2,2,128]{4,2,3,1,0:T(2,128)S(1)} %bitcast.168, s32[1024]{0:T(1024)S(1)} %pad_clamp_fusion.2), kind=kCustom, calls=%fused_computation.2.clone | custom fusion | bytes 5899008 | tf_op jit(solution)/shard_map/jit(_take)/gather | solution.py:143
  359.9 6.8 select_bitcast_fusion.1
  366.7 8.0 %copy.339 = f32[3,5,2,192,128]{3,2,4,1,0:T(2,128)} copy(f32[3,5,2,192,128]{4,2,1,0,3:T(2,128)} %get-tuple-element.469) | data formatting | bytes 5898240 | tf_op jit(solution)/shard_map/jit(_take)/select_n | solution.py:143
  374.6 11.1 %gather_fusion.5 = f32[96,3,5,2,192]{4,3,2,1,0:T(2,128)S(1)} fusion(f32[3,5,2,192,128]{3,2,4,1,0:T(2,128)} %copy.339, s32[1024]{0:T(1024)S(1)} %pad_clamp_fusion.1), kind=kCustom, calls=%fused_computation.3.clone | custom fusion | bytes 4424064 | tf_op jit(solution)/shard_map/jit(_take)/gather | solution.py:144
  419.1 12.1 %gather_fusion.3 = f32[192,3,5,2,96]{4,3,2,1,0:T(2,128)} fusion(f32[3,5,2,96,128]{3,2,4,1,0:T(2,128)S(1)} %copy.337, s32[1024]{0:T(1024)S(1)} %pad_clamp_fusion.4), kind=kCustom, calls=%fused_computation.7.clone | custom fusion | bytes 4424448 | tf_op jit(solution)/shard_map/jit(_take)/gather | solution.py:140
  431.3 14.2 %gather_fusion.1 = f32[192,3,5,2,96]{4,3,2,1,0:T(2,128)} fusion(f32[3,5,2,96,128]{3,2,4,1,0:T(2,128)} %copy.335, s32[1024]{0:T(1024)S(1)} %pad_clamp_fusion.4), kind=kCustom, calls=%fused_computation.1.clone | custom fusion | bytes 4424448 | tf_op jit(solution)/shard_map/jit(_take)/gather | solution.py:140
  445.5 9.3 %multiply_add_fusion.3 = f32[3,5,2,96,192]{3,2,1,0,4:T(2,128)S(1)} fusion(f32[3,5,2,96,192]{3,2,1,0,4:T(2,128)} %get-tuple-element.219, pred[3,96,192]{1,0,2:T(4,128)(4,1)S(1)} %copy-done.13, f32[96,3,5,2,192]{0,3,2,1,4:T(2,128)} %copy.343, pred[192]{0:T(512)(128)(4,1)S(1)} %copy-done.18, f32[96,3,5,2,192]{0,3,2,1,4:T(2,128)} %copy.340, ...), kind=kLoop, calls=%fused_computation.97 | loop fusion | flops 6635520 | bytes 13400928 | tf_op jit(solution)/shard_map/add | solution.py:177
  488.4 8.4 %select_maximum_fusion.4 = f32[3,5,4,98,194]{3,2,1,0,4:T(4,128)S(1)} fusion(f32[3,5,2,98,1]{3,2,1,0,4:T(2,128)S(1)} %collective-permute-done.14, f32[3,5,2,98,1]{3,2,1,0,4:T(2,128)S(1)} %collective-permute-done.15, f32[3,5,2,1,192]{3,2,1,0,4:T(2,128)S(1)} %copy-done.2, f32[3,5,2,96,192]{3,2,1,0,4:T(2,128)S(1)} %multiply_add_fusion.3, ...), kind=kLoop, calls=%fused_computation.41 | loop fusion | flops 13688640 | bytes 6844320 | tf_op jit(solution)/shard_map/concatenate | solution.py:17
  496.8 37.4 %multiply_add_fusion.2 = f32[3,5,2,96,192]{3,2,1,0,4:T(2,128)S(1)} fusion(f32[3,5,2,96,192]{3,2,1,0,4:T(2,128)S(1)} %multiply_add_fusion.3, f32[3,5,4,98,194]{3,2,1,0,4:T(4,128)S(1)} %select_maximum_fusion.4, f32[3,5,2,1,192]{3,2,1,0,4:T(2,128)S(1)} %copy-done.2, f32[3,5,2,1,192]{3,2,1,0,4:T(2,128)S(1)} %copy-done.4, ...), kind=kLoop, calls=%fused_computation.96 | loop fusion | flops 11612160 | bytes 8990728 | tf_op jit(solution)/shard_map/add | solution.py:181
  569.3 8.2 %copy.367 = f32[3,5,2,192,128]{3,2,4,1,0:T(2,128)} copy(f32[3,5,2,192,128]{4,2,1,0,3:T(2,128)} %get-tuple-element.470) | data formatting | bytes 5898240 | tf_op jit(solution)/shard_map/jit(_take)/select_n | solution.py:143
  577.5 10.8 %gather_fusion.15 = f32[96,3,5,2,192]{4,3,2,1,0:T(2,128)} fusion(f32[3,5,2,192,128]{3,2,4,1,0:T(2,128)} %copy.367, s32[1024]{0:T(1024)S(1)} %pad_clamp_fusion.1), kind=kCustom, calls=%fused_computation.15.clone | custom fusion | bytes 4424064 | tf_op jit(solution)/shard_map/jit(_take)/gather | solution.py:144
  588.3 7.3 copy.368
  595.6 8.0 %copy.364 = f32[3,5,2,192,128]{3,2,4,1,0:T(2,128)} copy(f32[3,5,2,192,128]{4,2,1,0,3:T(2,128)} %get-tuple-element.468) | data formatting | bytes 5898240 | tf_op jit(solution)/shard_map/jit(_take)/select_n | solution.py:143
  603.6 10.8 %gather_fusion.13 = f32[96,3,5,2,192]{4,3,2,1,0:T(2,128)} fusion(f32[3,5,2,192,128]{3,2,4,1,0:T(2,128)} %copy.364, s32[1024]{0:T(1024)S(1)} %pad_clamp_fusion.1), kind=kCustom, calls=%fused_computation.14.clone | custom fusion | bytes 4424064 | tf_op jit(solution)/shard_map/jit(_take)/gather | solution.py:144
  614.3 7.3 copy.365
  626.1 14.1 %gather_fusion.11 = f32[192,3,5,2,96]{4,3,2,1,0:T(2,128)} fusion(f32[3,5,2,96,128]{3,2,4,1,0:T(2,128)} %copy.362, s32[1024]{0:T(1024)S(1)} %pad_clamp_fusion.4), kind=kCustom, calls=%fused_computation.9.clone | custom fusion | bytes 4424448 | tf_op jit(solution)/shard_map/jit(_take)/gather | solution.py:140
  644.7 13.6 %gather_fusion.9 = f32[192,3,5,2,96]{4,3,2,1,0:T(2,128)} fusion(f32[3,5,2,96,128]{3,2,4,1,0:T(2,128)} %copy.360, s32[1024]{0:T(1024)S(1)} %pad_clamp_fusion.4), kind=kCustom, calls=%fused_computation.8.clone | custom fusion | bytes 4424448 | tf_op jit(solution)/shard_map/jit(_take)/gather | solution.py:140
  658.4 9.2 %pad_maximum_fusion.1 = f32[3,5,2,108,204]{3,2,1,0,4:T(2,128)} fusion(f32[3,5,2,108,6]{3,2,1,0,4:T(2,128)S(1)} %collective-permute-done.19, f32[3,5,2,6,192]{3,2,1,0,4:T(2,128)} %copy.354, f32[3,5,2,96,192]{3,2,1,0,4:T(2,128)S(1)} %copy-done.1, f32[3,5,2,6,192]{3,2,1,0,4:T(2,128)} %copy.353, f32[3,5,2,108,6]{3,2,1,0,4:T(2,128)} %collective-permute-done.18), kind=kLoop, calls=%fused_computation.47 | loop fusion | flops 2643840 | bytes 5287680 | tf_op jit(solution)/shard_map/concatenate | solution.py:17
  668.5 18.0 %while.35 = (s32[]{:T(128)}, f32[3,5,2,108,204]{3,2,1,0,4:T(2,128)}, s32[3,5]{1,0:T(4,128)}, f32[3,5,2,96,192]{3,2,1,0,4:T(2,128)S(1)}, s32[]{:T(128)}) while((s32[]{:T(128)}, f32[3,5,2,108,204]{3,2,1,0,4:T(2,128)}, s32[3,5]{1,0:T(4,128)}, f32[3,5,2,96,192]{3,2,1,0,4:T(2,128)S(1)}, s32[]{:T(128)}) %tuple.221), condition=%wide.while_cond.1, body=%wide.while_body.1.sunk | while | flops 2 | bytes 1720473 | solution.py:132
  688.1 9.3 %multiply_add_fusion.1 = f32[3,5,2,96,192]{3,2,1,0,4:T(2,128)S(1)} fusion(f32[3,5,2,96,192]{3,2,1,0,4:T(2,128)} %copy-done.7, pred[3,96,192]{1,0,2:T(4,128)(4,1)S(1)} %broadcast_and_fusion.1, f32[96,3,5,2,192]{0,3,2,1,4:T(2,128)} %copy.368, pred[192]{0:T(512)(128)(4,1)S(1)} %copy-done.19, f32[96,3,5,2,192]{0,3,2,1,4:T(2,128)} %copy.365, ...), kind=kLoop, calls=%fused_computation.95 | loop fusion | flops 6635520 | bytes 13400928 | tf_op jit(solution)/shard_map/add | solution.py:177
  731.0 8.4 %select_maximum_fusion = f32[3,5,4,98,194]{3,2,1,0,4:T(4,128)S(1)} fusion(f32[3,5,2,98,1]{3,2,1,0,4:T(2,128)S(1)} %collective-permute-done.22, f32[3,5,2,98,1]{3,2,1,0,4:T(2,128)S(1)} %collective-permute-done.23, f32[3,5,2,1,192]{3,2,1,0,4:T(2,128)S(1)} %copy-done.3, f32[3,5,2,96,192]{3,2,1,0,4:T(2,128)S(1)} %multiply_add_fusion.1, ...), kind=kLoop, calls=%fused_computation.37 | loop fusion | flops 13688640 | bytes 6844320 | tf_op jit(solution)/shard_map/concatenate | solution.py:17
  739.4 38.3 %multiply_add_fusion = f32[3,5,2,96,192]{3,2,1,0,4:T(2,128)} fusion(f32[3,5,2,96,192]{3,2,1,0,4:T(2,128)S(1)} %multiply_add_fusion.1, f32[3,5,4,98,194]{3,2,1,0,4:T(4,128)S(1)} %select_maximum_fusion, f32[3,5,2,1,192]{3,2,1,0,4:T(2,128)S(1)} %copy-done.3, f32[3,5,2,1,192]{3,2,1,0,4:T(2,128)S(1)} %copy-done.5, ...), kind=kLoop, calls=%fused_computation.94 | loop fusion | flops 11612160 | bytes 8990728 | tf_op jit(solution)/shard_map/add | solution.py:181
  (376 shorter events, 332.0 us)
Async XLA Ops:
  7.2 33.1 %copy-start.8 = (f32[5,2,64,128]{3,2,1,0:T(8,128)S(1)}, f32[5,2,64,128]{3,2,1,0:T(8,128)}, u32[]{:S(2)}) copy-start(f32[5,2,64,128]{3,2,1,0:T(8,128)} %param.18) | copy-start | bytes 983044
  7.2 273.9 %all-reduce.9.cloned.1.call-start = ((), (), s32[]{:S(2)}) async-start(), calls=%async_computation | async-start | bytes 983040 | tf_op jit(solution)/shard_map/psum | solution.py:157
  8.1 25.3 %collective-permute-start = (f32[5,2,1,128]{3,2,1,0:T(1,128)S(1)}, f32[5,2,1,128]{3,2,1,0:T(1,128)S(1)}, u32[]{:S(2)}, u32[]{:S(2)}) collective-permute-start(f32[5,2,1,128]{3,2,1,0:T(1,128)S(1)} %get-tuple-element.438), channel_id=1, source_target_pairs={{4,0},{8,4},{12,8},{5,1},{9,5},{13,9},{6,2},{10,6},{14,10},{7,3},{... | collective-permute-start | bytes 15368 | tf_op jit(solution)/shard_map/ppermute | solution.py:21
  9.4 24.0 %collective-permute-start.1 = (f32[5,2,1,128]{3,2,1,0:T(1,128)S(1)}, f32[5,2,1,128]{3,2,1,0:T(1,128)S(1)}, u32[]{:S(2)}, u32[]{:S(2)}) collective-permute-start(f32[5,2,1,128]{3,2,1,0:T(1,128)S(1)} %get-tuple-element.437), channel_id=1, source_target_pairs={{0,4},{4,8},{8,12},{1,5},{5,9},{9,13},{2,6},{6,10},{10,14},{3,7},{... | collective-permute-start | bytes 15368 | tf_op jit(solution)/shard_map/ppermute | solution.py:19
  16.1 24.5 %copy-start.14 = (f32[5]{0:T(128)S(1)}, f32[5]{0:T(128)}, u32[]{:S(2)}) copy-start(f32[5]{0:T(128)} %param.21) | copy-start | bytes 64
  16.2 24.5 %copy-start.15 = (f32[5]{0:T(128)S(1)}, f32[5]{0:T(128)}, u32[]{:S(2)}) copy-start(f32[5]{0:T(128)} %param.20) | copy-start | bytes 64
  16.2 102.9 %collective-permute-start.9 = (f32[3,5,2,6,192]{4,2,3,1,0:T(2,128)S(1)}, f32[3,5,2,6,192]{4,2,3,1,0:T(2,128)}, u32[]{:S(2)}, u32[]{:S(2)}) collective-permute-start(f32[3,5,2,6,192]{4,2,3,1,0:T(2,128)S(1)} %copy.384), channel_id=1, source_target_pairs={{4,0},{8,4},{12,8},{5,1},{9,5},{13,9},{6,2},{10,6},{14,10},{7,3},{... | collective-permute-start | bytes 414728 | tf_op jit(solution)/shard_map/ppermute | solution.py:21
  18.3 105.0 %collective-permute-start.8 = (f32[3,5,2,6,192]{4,2,3,1,0:T(2,128)}, f32[3,5,2,6,192]{4,2,3,1,0:T(2,128)}, u32[]{:S(2)}, u32[]{:S(2)}) collective-permute-start(f32[3,5,2,6,192]{4,2,3,1,0:T(2,128)} %copy.383), channel_id=1, source_target_pairs={{0,4},{4,8},{8,12},{1,5},{5,9},{9,13},{2,6},{6,10},{10,14},{3,7},{... | collective-permute-start | bytes 414728 | tf_op jit(solution)/shard_map/ppermute | solution.py:19
  34.6 4.4 collective-permute-start.2
  35.9 4.3 collective-permute-start.3
  39.0 406.5 %copy-start.24 = (pred[192]{0:T(512)(128)(4,1)}, pred[192]{0:T(512)(128)(4,1)S(1)}, u32[]{:S(2)}) copy-start(pred[192]{0:T(512)(128)(4,1)S(1)} %broadcast_compare_fusion.1) | copy-start | bytes 580
  41.3 14.7 %collective-permute-start.4 = (f32[5,2,1,128]{3,2,1,0:T(1,128)S(1)}, f32[5,2,1,128]{3,2,1,0:T(1,128)S(1)}, u32[]{:S(2)}, u32[]{:S(2)}) collective-permute-start(f32[5,2,1,128]{3,2,1,0:T(1,128)S(1)} %get-tuple-element.436), channel_id=1, source_target_pairs={{4,0},{8,4},{12,8},{5,1},{9,5},{13,9},{6,2},{10,6},{14,10},{7,3},{... | collective-permute-start | bytes 15368 | tf_op jit(solution)/shard_map/ppermute | solution.py:21
  42.6 13.4 %collective-permute-start.5 = (f32[5,2,1,128]{3,2,1,0:T(1,128)S(1)}, f32[5,2,1,128]{3,2,1,0:T(1,128)S(1)}, u32[]{:S(2)}, u32[]{:S(2)}) collective-permute-start(f32[5,2,1,128]{3,2,1,0:T(1,128)S(1)} %get-tuple-element.435), channel_id=1, source_target_pairs={{0,4},{4,8},{8,12},{1,5},{5,9},{9,13},{2,6},{6,10},{10,14},{3,7},{... | collective-permute-start | bytes 15368 | tf_op jit(solution)/shard_map/ppermute | solution.py:19
  47.2 398.3 %copy-start.26 = (pred[96]{0:T(512)(128)(4,1)}, pred[96]{0:T(512)(128)(4,1)S(1)}, u32[]{:S(2)}) copy-start(pred[96]{0:T(512)(128)(4,1)S(1)} %broadcast_compare_fusion.3) | copy-start | bytes 292
  56.9 57.3 %collective-permute-start.6 = (f32[5,2,66,1]{3,2,1,0:T(8,128)}, f32[5,2,66,1]{3,2,1,0:T(8,128)S(1)}, u32[]{:S(2)}, u32[]{:S(2)}) collective-permute-start(f32[5,2,66,1]{3,2,1,0:T(8,128)} %get-tuple-element.432), channel_id=1, source_target_pairs={{1,0},{2,1},{3,2},{5,4},{6,5},{7,6},{9,8},{10,9},{11,10},{13,12},{... | collective-permute-start | bytes 7928 | tf_op jit(solution)/shard_map/ppermute | solution.py:21
  58.2 56.0 %collective-permute-start.7 = (f32[5,2,66,1]{3,2,1,0:T(8,128)S(1)}, f32[5,2,66,1]{3,2,1,0:T(8,128)S(1)}, u32[]{:S(2)}, u32[]{:S(2)}) collective-permute-start(f32[5,2,66,1]{3,2,1,0:T(8,128)S(1)} %get-tuple-element.431), channel_id=1, source_target_pairs={{0,1},{1,2},{2,3},{4,5},{5,6},{6,7},{8,9},{9,10},{10,11},{12,13},{... | collective-permute-start | bytes 7928 | tf_op jit(solution)/shard_map/ppermute | solution.py:19
  129.4 57.4 %collective-permute-start.11 = (f32[3,5,2,108,6]{3,2,4,1,0:T(2,128)}, f32[3,5,2,108,6]{3,2,4,1,0:T(2,128)S(1)}, u32[]{:S(2)}, u32[]{:S(2)}) collective-permute-start(f32[3,5,2,108,6]{3,2,4,1,0:T(2,128)} %get-tuple-element.422), channel_id=1, source_target_pairs={{1,0},{3,2},{5,4},{7,6},{9,8},{11,10},{13,12},{15,14},{17,16},{19,... | collective-permute-start | bytes 233288 | tf_op jit(solution)/shard_map/ppermute | solution.py:21
  130.7 56.1 %collective-permute-start.10 = (f32[3,5,2,108,6]{3,2,4,1,0:T(2,128)S(1)}, f32[3,5,2,108,6]{3,2,4,1,0:T(2,128)}, u32[]{:S(2)}, u32[]{:S(2)}) collective-permute-start(f32[3,5,2,108,6]{3,2,4,1,0:T(2,128)S(1)} %get-tuple-element.421), channel_id=1, source_target_pairs={{0,1},{2,3},{4,5},{6,7},{8,9},{10,11},{12,13},{14,15},{16,17},{18,... | collective-permute-start | bytes 233288 | tf_op jit(solution)/shard_map/ppermute | solution.py:19
  465.5 9.9 %collective-permute-start.12 = (f32[3,5,2,1,192]{4,2,3,1,0:T(2,128)S(1)}, f32[3,5,2,1,192]{4,2,3,1,0:T(2,128)S(1)}, u32[]{:S(2)}, u32[]{:S(2)}) collective-permute-start(f32[3,5,2,1,192]{4,2,3,1,0:T(2,128)S(1)} %copy.345), channel_id=1, source_target_pairs={{4,0},{8,4},{12,8},{5,1},{9,5},{13,9},{6,2},{10,6},{14,10},{7,3},{... | collective-permute-start | bytes 69128 | tf_op jit(solution)/shard_map/ppermute | solution.py:21
  470.8 7.8 collective-permute-start.13
  483.1 4.6 collective-permute-start.14
  484.6 3.9 collective-permute-start.15
  543.8 10.6 %collective-permute-start.17 = (f32[3,5,2,6,192]{4,2,3,1,0:T(2,128)S(1)}, f32[3,5,2,6,192]{4,2,3,1,0:T(2,128)S(1)}, u32[]{:S(2)}, u32[]{:S(2)}) collective-permute-start(f32[3,5,2,6,192]{4,2,3,1,0:T(2,128)S(1)} %copy.352), channel_id=1, source_target_pairs={{4,0},{8,4},{12,8},{5,1},{9,5},{13,9},{6,2},{10,6},{14,10},{7,3},{... | collective-permute-start | bytes 414728 | tf_op jit(solution)/shard_map/ppermute | solution.py:21
  548.4 9.3 %collective-permute-start.16 = (f32[3,5,2,6,192]{4,2,3,1,0:T(2,128)}, f32[3,5,2,6,192]{4,2,3,1,0:T(2,128)}, u32[]{:S(2)}, u32[]{:S(2)}) collective-permute-start(f32[3,5,2,6,192]{4,2,3,1,0:T(2,128)} %copy.351), channel_id=1, source_target_pairs={{0,4},{4,8},{8,12},{1,5},{5,9},{9,13},{2,6},{6,10},{10,14},{3,7},{... | collective-permute-start | bytes 414728 | tf_op jit(solution)/shard_map/ppermute | solution.py:19
  564.1 94.3 %collective-permute-start.19 = (f32[3,5,2,108,6]{3,2,1,0,4:T(2,128)}, f32[3,5,2,108,6]{3,2,1,0,4:T(2,128)S(1)}, u32[]{:S(2)}, u32[]{:S(2)}) collective-permute-start(f32[3,5,2,108,6]{3,2,1,0,4:T(2,128)} %get-tuple-element.418), channel_id=1, source_target_pairs={{1,0},{3,2},{5,4},{7,6},{9,8},{11,10},{13,12},{15,14},{17,16},{19,... | collective-permute-start | bytes 233288 | tf_op jit(solution)/shard_map/ppermute | solution.py:21
  565.4 93.0 %collective-permute-start.18 = (f32[3,5,2,108,6]{3,2,1,0,4:T(2,128)S(1)}, f32[3,5,2,108,6]{3,2,1,0,4:T(2,128)}, u32[]{:S(2)}, u32[]{:S(2)}) collective-permute-start(f32[3,5,2,108,6]{3,2,1,0,4:T(2,128)S(1)} %get-tuple-element.417), channel_id=1, source_target_pairs={{0,1},{2,3},{4,5},{6,7},{8,9},{10,11},{12,13},{14,15},{16,17},{18,... | collective-permute-start | bytes 233288 | tf_op jit(solution)/shard_map/ppermute | solution.py:19
  668.4 19.6 %copy-start.17 = (pred[192]{0:T(512)(128)(4,1)S(1)}, pred[192]{0:T(512)(128)(4,1)}, u32[]{:S(2)}) copy-start(pred[192]{0:T(512)(128)(4,1)} %get-tuple-element.492) | copy-start | bytes 580
  668.4 19.6 %copy-start.19 = (pred[192]{0:T(512)(128)(4,1)S(1)}, pred[192]{0:T(512)(128)(4,1)}, u32[]{:S(2)}) copy-start(pred[192]{0:T(512)(128)(4,1)} %get-tuple-element.493) | copy-start | bytes 580
  707.9 10.0 %collective-permute-start.20 = (f32[3,5,2,1,192]{4,2,3,1,0:T(2,128)S(1)}, f32[3,5,2,1,192]{4,2,3,1,0:T(2,128)S(1)}, u32[]{:S(2)}, u32[]{:S(2)}) collective-permute-start(f32[3,5,2,1,192]{4,2,3,1,0:T(2,128)S(1)} %copy.370), channel_id=1, source_target_pairs={{4,0},{8,4},{12,8},{5,1},{9,5},{13,9},{6,2},{10,6},{14,10},{7,3},{... | collective-permute-start | bytes 69128 | tf_op jit(solution)/shard_map/ppermute | solution.py:21
  713.2 8.0 %collective-permute-start.21 = (f32[3,5,2,1,192]{4,2,3,1,0:T(2,128)S(1)}, f32[3,5,2,1,192]{4,2,3,1,0:T(2,128)S(1)}, u32[]{:S(2)}, u32[]{:S(2)}) collective-permute-start(f32[3,5,2,1,192]{4,2,3,1,0:T(2,128)S(1)} %copy.372), channel_id=1, source_target_pairs={{0,4},{4,8},{8,12},{1,5},{5,9},{9,13},{2,6},{6,10},{10,14},{3,7},{... | collective-permute-start | bytes 69128 | tf_op jit(solution)/shard_map/ppermute | solution.py:19
  725.7 4.5 collective-permute-start.22
  727.1 3.9 collective-permute-start.23
  (28 other events, 279.9 us)
Sparse Core Ops, SparseCore 0:
  187.0 94.0 all-reduce.8
where the time goes:
time: 801 us; the launch traced here: 790 us
  local copies, waits for them, and re-layouts  416 us (52%)
  other arithmetic  168 us (21%)
  waiting for transfers between devices  73.1 us (9%)
  starting transfers between devices  70.8 us (9%)
  loops' own time  46.6 us (6%)
  between operations  15.3 us (2%)
    add x2, other arithmetic, per_device(): nests_now = relaxed + inside * change  75.6 us
    psum x1, waiting for transfers between devices, per_device(): totals = lax.psum(terms, ('tile', 'nest', 'lev'))  70.3 us
    gather x8, local copies, waits for them, and re-layouts, along(): picked = jnp.take(picked, coarse_rows, axis=4)  68.6 us
    ppermute x12, starting transfers between devices, extended(): lax.ppermute(tail, axis, [(i, (i + 1) % count) for i in range(ends)])  55 us
    gather x4, local copies, waits for them, and re-layouts, across(): return jnp.take(picked, coarse_cols, axis=4)  54 us
    another operation x2, loops' own time, extract(): return lax.map(single, corners)  46.6 us
    gather x4, local copies, waits for them, and re-layouts, along(): picked = jnp.take(zone, zone_index, axis=3)  46.3 us
    concatenate x10, other arithmetic, extended(): jnp.concatenate([lax.ppermute(tail, axis, [(i, (i + 1) % count) for i in...  38.2 us
  transfers between devices with their start and end apart: 25, of which 4 were waited for; matrix products, arithmetic and copies ran while one was open for 28% of the time, Pallas kernels for 0%

commit v1 on v0

--- a/solution.py
+++ b/solution.py
@@ -154,7 +154,7 @@
         later_pos = select_rows(pick_all, centres[step_index + 1])
         anchors = later_pos - FP // 2
         terms = extract(parent_now, anchors)
-        totals = lax.psum(terms, ("tile", "nest", "lev"))
+        totals = jnp.sum(lax.all_gather(terms, ("tile", "nest", "lev")), axis=0)
         boundary = lax.dynamic_slice_in_dim(totals, nest_at * slot_count, slot_count, 0)
         boundary = boundary.reshape(slot_count, fields, level_count, 4, BWP, FP)
         south_full = across(boundary[:, :, :, 0], south_index)

time: 801 us -> 703 us (0.88)
  waiting for transfers between devices: 73.1 us -> 5.48 us
  other arithmetic: 168 us -> 142 us
  local copies, waits for them, and re-layouts: 416 us -> 404 us
    psum x1 -> x0, waiting for transfers between devices: 70.3 us -> none  [per_device(): totals = lax.psum(terms, ('tile', 'nest', 'lev'))]
    add x2, other arithmetic: 75.6 us -> 50.2 us  [per_device(): nests_now = relaxed + inside * change]
    gather x4, local copies, waits for them, and re-layouts: 54 us -> 33 us  [across(): return jnp.take(picked, coarse_cols, axis=4)]
    gather x1 -> x3, local copies, waits for them, and re-layouts: 0.08 us -> 12.1 us  [relocate(): lax.dynamic_slice(single, (zero_index, zero_index, reach_rows + offset[0]...]
    gather x18 -> x24, local copies, waits for them, and re-layouts: 31.2 us -> 36.3 us
    unnamed x87 -> x118, local copies, waits for them, and re-layouts: 18.4 us -> 20 us
  transfers between devices with their start and end apart: 25 -> 26, of which waited for: 4 -> 7; matrix products, arithmetic and copies ran while one was open for 28% -> 28% of each run, Pallas kernels for 0% -> 0%
where the time goes in v1:
time: 703 us; the launch traced here: 691 us
  local copies, waits for them, and re-layouts  404 us (57%)
  other arithmetic  142 us (20%)
  starting transfers between devices  75.8 us (11%)
  loops' own time  47.7 us (7%)
  between operations  15.4 us (2%)
    gather x8, local copies, waits for them, and re-layouts, along(): picked = jnp.take(picked, coarse_rows, axis=4)  66.7 us
    ppermute x12, starting transfers between devices, extended(): lax.ppermute(tail, axis, [(i, (i + 1) % count) for i in range(ends)])  59.6 us
    add x2, other arithmetic, per_device(): nests_now = relaxed + inside * change  50.2 us
    another operation x2, loops' own time, extract(): return lax.map(single, corners)  47.7 us
    gather x4, local copies, waits for them, and re-layouts, along(): picked = jnp.take(zone, zone_index, axis=3)  46.2 us
    gather x24, local copies, waits for them, and re-layouts  36.3 us
    slice x11, local copies, waits for them, and re-layouts, extended(): lax.slice_in_dim(cells, cells.shape[dim] - width, cells.shape[dim], axis=...  33.2 us
    gather x4, local copies, waits for them, and re-layouts, across(): return jnp.take(picked, coarse_cols, axis=4)  33 us
  transfers between devices with their start and end apart: 26, of which 7 were waited for; matrix products, arithmetic and copies ran while one was open for 28% of the time, Pallas kernels for 0%

profile of v1, /device:TPU:0, one launch (start us, length us, event | category | flops | bytes accessed | tf_op | source)
XLA Modules:
  0.0 690.9 jit_solution(16137449762624660267)
XLA Ops:
  29.2 50.2 %while.32 = (s32[]{:T(128)}, f32[6,5,2,1024]{3,2,1,0:T(2,128)S(1)}, s32[6,2]{0,1:T(2,128)S(1)}, f32[5,2,320,384]{2,3,1,0:T(8,128)}, s32[]{:T(128)}, /*index=5*/s...) while((s32[]{:T(128)}, f32[6,5,2,1024]{3,2,1,0:T(2,128)S(1)}, ...), condition=%wide.region_5.6_spmd, body=%wide.region_4.5_spmd.sunk | while | flops 40981 | bytes 450935 | solution.py:92
  89.8 6.1 collective-permute-start.7
  101.6 50.0 %while.33 = (s32[]{:T(128)}, f32[6,5,2,1024]{3,2,1,0:T(2,128)S(1)}, s32[6,2]{0,1:T(2,128)S(1)}, f32[5,2,320,384]{2,3,1,0:T(8,128)}, s32[]{:T(128)}, /*index=5*/s...) while((s32[]{:T(128)}, f32[6,5,2,1024]{3,2,1,0:T(2,128)S(1)}, ...), condition=%wide.region_9.14_spmd, body=%wide.region_8.13_spmd.sunk | while | flops 40981 | bytes 450935 | solution.py:92
  182.9 10.1 %collective-permute-start.10 = (f32[3,5,2,108,6]{3,2,4,1,0:T(2,128)S(1)}, f32[3,5,2,108,6]{3,2,4,1,0:T(2,128)S(1)}, u32[]{:S(2)}, u32[]{:S(2)}) collective-permute-start(f32[3,5,2,108,6]{3,2,4,1,0:T(2,128)S(1)} %get-tuple-element.419), channel_id=1, source_target_pairs={{0,1},{2,3},{4,5},{6,7},{8,9},{10,11},{12,13},{14,15},{16,17},{18,... | collective-permute-start | bytes 233288 | tf_op jit(solution)/shard_map/ppermute | solution.py:19
  193.8 7.4 %pad_maximum_fusion.17 = f32[3,5,2,108,204]{3,2,4,1,0:T(2,128)} fusion(f32[3,5,2,108,6]{3,2,4,1,0:T(2,128)S(1)} %collective-permute-done.11, f32[3,5,2,6,192]{3,2,4,1,0:T(2,128)S(1)} %copy-done.6, f32[3,5,2,96,192]{3,2,4,1,0:T(2,128)S(1)} %copy.340, f32[3,5,2,6,192]{3,2,4,1,0:T(2,128)S(1)} %copy-done.7, f32[3,5,2,108,6]{3,2,4,1,0:T(2,128)S(1)} %collective-permute-done.10), kind=kLoop, calls=%fused_computation.97 | loop fusion | flops 2643840 | bytes 5287680 | tf_op jit(solution)/shard_map/concatenate | solution.py:17
  203.1 22.5 %while.34 = (s32[]{:T(128)}, f32[3,5,2,108,204]{3,2,4,1,0:T(2,128)}, s32[3,5]{1,0:T(4,128)}, f32[3,5,2,96,192]{4,3,2,1,0:T(8,128)}, s32[]{:T(128)}) while((s32[]{:T(128)}, f32[3,5,2,108,204]{3,2,4,1,0:T(2,128)}, s32[3,5]{1,0:T(4,128)}, f32[3,5,2,96,192]{4,3,2,1,0:T(8,128)}, s32[]{:T(128)}) %tuple.212), condition=%wide.while_cond, body=%wide.while_body.sunk | while | flops 2 | bytes 4669593 | solution.py:132
  225.7 5.9 copy.357
  239.0 12.4 %gather_fusion.14 = f32[192,3,5,2,128]{4,3,2,1,0:T(2,128)S(1)} fusion(f32[3,5,2,2,128]{4,2,3,1,0:T(2,128)S(1)} %bitcast.168, s32[1024]{0:T(1024)S(1)} %pad_clamp_fusion), kind=kCustom, calls=%fused_computation.12.clone | custom fusion | bytes 5899008 | tf_op jit(solution)/shard_map/jit(_take)/gather | solution.py:143
  251.5 11.0 %gather_fusion.6 = f32[192,3,5,2,128]{4,3,2,1,0:T(2,128)} fusion(f32[3,5,2,2,128]{4,2,3,1,0:T(2,128)S(1)} %bitcast.169, s32[1024]{0:T(1024)S(1)} %pad_clamp_fusion), kind=kCustom, calls=%fused_computation.10.clone | custom fusion | bytes 5899008 | tf_op jit(solution)/shard_map/jit(_take)/gather | solution.py:143
  262.5 6.9 select_bitcast_fusion
  269.4 8.0 %copy.355 = f32[3,5,2,192,128]{3,2,4,1,0:T(2,128)} copy(f32[3,5,2,192,128]{4,2,1,0,3:T(2,128)} %get-tuple-element.471) | data formatting | bytes 5898240 | tf_op jit(solution)/shard_map/jit(_take)/select_n | solution.py:143
  277.3 11.4 %gather_fusion.7 = f32[96,3,5,2,192]{4,3,2,1,0:T(2,128)S(1)} fusion(f32[3,5,2,192,128]{3,2,4,1,0:T(2,128)} %copy.355, s32[1024]{0:T(1024)S(1)} %pad_clamp_fusion.1), kind=kCustom, calls=%fused_computation.13.clone | custom fusion | bytes 4424064 | tf_op jit(solution)/shard_map/jit(_take)/gather | solution.py:144
  294.0 11.8 %gather_fusion.12 = f32[192,3,5,2,128]{4,3,2,1,0:T(2,128)S(1)} fusion(f32[3,5,2,2,128]{4,2,3,1,0:T(2,128)S(1)} %bitcast.171, s32[1024]{0:T(1024)S(1)} %pad_clamp_fusion.2), kind=kCustom, calls=%fused_computation.11.clone | custom fusion | bytes 5899008 | tf_op jit(solution)/shard_map/jit(_take)/gather | solution.py:143
  305.9 10.9 %gather_fusion.4 = f32[192,3,5,2,128]{4,3,2,1,0:T(2,128)} fusion(f32[3,5,2,2,128]{4,2,3,1,0:T(2,128)S(1)} %bitcast.170, s32[1024]{0:T(1024)S(1)} %pad_clamp_fusion.2), kind=kCustom, calls=%fused_computation.2.clone | custom fusion | bytes 5899008 | tf_op jit(solution)/shard_map/jit(_take)/gather | solution.py:143
  316.7 6.9 select_bitcast_fusion.1
  323.6 8.0 %copy.352 = f32[3,5,2,192,128]{3,2,4,1,0:T(2,128)} copy(f32[3,5,2,192,128]{4,2,1,0,3:T(2,128)} %get-tuple-element.469) | data formatting | bytes 5898240 | tf_op jit(solution)/shard_map/jit(_take)/select_n | solution.py:143
  331.6 11.0 %gather_fusion.5 = f32[96,3,5,2,192]{4,3,2,1,0:T(2,128)S(1)} fusion(f32[3,5,2,192,128]{3,2,4,1,0:T(2,128)} %copy.352, s32[1024]{0:T(1024)S(1)} %pad_clamp_fusion.1), kind=kCustom, calls=%fused_computation.3.clone | custom fusion | bytes 4424064 | tf_op jit(solution)/shard_map/jit(_take)/gather | solution.py:144
  376.6 12.3 %gather_fusion.3 = f32[192,3,5,2,96]{4,3,2,1,0:T(2,128)} fusion(f32[3,5,2,96,128]{3,2,4,1,0:T(2,128)S(1)} %copy.349, s32[1024]{0:T(1024)S(1)} %pad_clamp_fusion.4), kind=kCustom, calls=%fused_computation.7.clone | custom fusion | bytes 4424448 | tf_op jit(solution)/shard_map/jit(_take)/gather | solution.py:140
  394.0 7.7 %multiply_add_fusion.1 = f32[3,5,2,96,192]{3,1,2,0,4:T(8,128)S(1)} fusion(f32[3,5,2,96,192]{3,1,2,0,4:T(8,128)} %copy.357, f32[96,3,5,2,192]{0,2,3,1,4:T(8,128)} %copy.356, f32[96,3,5,2,192]{0,2,3,1,4:T(8,128)} %copy.353, f32[192,3,5,2,96]{4,3,2,1,0:T(2,128)S(1)} %copy-done.9, f32[192,3,5,2,96]{4,2,3,1,0:T(8,128)} %gather_fusion.1, ...), kind=kLoop, calls=%fused_computation.96 | loop fusion | flops 6635520 | bytes 13400928 | tf_op jit(solution)/shard_map/add | solution.py:177
  440.3 24.9 %fusion.15 = f32[3,5,2,96,192]{3,1,2,0,4:T(8,128)} fusion(f32[3,5,2,96,192]{3,1,2,0,4:T(8,128)S(1)} %bitcast.175, f32[3,5,4,98,194]{3,1,2,0,4:T(8,128)} %select_maximum_fusion.4, f32[3,5,2,98,1]{3,1,2,0,4:T(8,128)S(1)} %collective-permute-done.15, f32[3,5,2,1,192]{3,1,2,0,4:T(8,128)} %copy.359, f32[3,5,2,1,192]{3,1,2,0,4:T(8,128)} %copy.361, ...), kind=kLoop, calls=%fused_computation.71 | loop fusion | flops 11612160 | bytes 8990728 | tf_op jit(solution)/shard_map/add | solution.py:181
  465.2 8.9 %fusion.59 = (f32[3,5,2,6,192]{3,1,2,0,4:T(8,128)}, f32[3,5,2,6,192]{3,1,2,0,4:T(8,128)}) fusion(f32[3,5,2,96,192]{3,1,2,0,4:T(8,128)} %fusion.15), kind=kLoop, calls=%fused_computation.263 | loop fusion | bytes 552960 | tf_op jit(solution)/shard_map/slice | solution.py:16
  503.8 6.1 copy.381
  510.0 10.7 %gather_fusion.15 = f32[96,3,5,2,192]{4,3,2,1,0:T(2,128)} fusion(f32[3,5,2,192,128]{3,2,4,1,0:T(2,128)} %copy.381, s32[1024]{0:T(1024)S(1)} %pad_clamp_fusion.1), kind=kCustom, calls=%fused_computation.15.clone | custom fusion | bytes 4424064 | tf_op jit(solution)/shard_map/jit(_take)/gather | solution.py:144
  520.7 6.8 copy.382
  527.4 5.8 copy.378
  533.3 11.0 %gather_fusion.13 = f32[96,3,5,2,192]{4,3,2,1,0:T(2,128)S(1)} fusion(f32[3,5,2,192,128]{3,2,4,1,0:T(2,128)} %copy.378, s32[1024]{0:T(1024)S(1)} %pad_clamp_fusion.1), kind=kCustom, calls=%fused_computation.14.clone | custom fusion | bytes 4424064 | tf_op jit(solution)/shard_map/jit(_take)/gather | solution.py:144
  553.0 12.5 %gather_fusion.11 = f32[192,3,5,2,96]{4,3,2,1,0:T(2,128)} fusion(f32[3,5,2,96,128]{3,2,4,1,0:T(2,128)S(1)} %copy.375, s32[1024]{0:T(1024)S(1)} %pad_clamp_fusion.4), kind=kCustom, calls=%fused_computation.9.clone | custom fusion | bytes 4424448 | tf_op jit(solution)/shard_map/jit(_take)/gather | solution.py:140
  571.7 8.0 %pad_maximum_fusion = f32[3,5,2,108,204]{3,1,2,0,4:T(8,128)} fusion(f32[3,5,2,108,6]{3,1,2,0,4:T(8,128)S(1)} %collective-permute-done.19, f32[3,5,2,6,192]{3,1,2,0,4:T(8,128)} %copy.367, f32[3,5,2,96,192]{3,1,2,0,4:T(8,128)} %fusion.15, f32[3,5,2,6,192]{3,1,2,0,4:T(8,128)} %copy.366, f32[3,5,2,108,6]{3,1,2,0,4:T(8,128)} %collective-permute-done.18), kind=kLoop, calls=%fused_computation.46 | loop fusion | flops 2643840 | bytes 5287680 | tf_op jit(solution)/shard_map/concatenate | solution.py:17
  585.7 13.8 %while.35 = (s32[]{:T(128)}, f32[3,5,2,108,204]{4,3,2,1,0:T(8,128)S(1)}, s32[3,5]{1,0:T(4,128)}, f32[3,5,2,96,192]{4,3,2,1,0:T(8,128)}, s32[]{:T(128)}) while((s32[]{:T(128)}, f32[3,5,2,108,204]{4,3,2,1,0:T(8,128)S(1)}, s32[3,5]{1,0:T(4,128)}, f32[3,5,2,96,192]{4,3,2,1,0:T(8,128)}, s32[]{:T(128)}) %tuple.221), condition=%wide.while_cond.1, body=%wide.while_body.1.sunk | while | flops 2 | bytes 1721997 | solution.py:132
  599.6 6.1 copy.383
  605.7 7.7 %multiply_add_fusion = f32[3,5,2,96,192]{3,1,2,0,4:T(8,128)S(1)} fusion(f32[3,5,2,96,192]{3,1,2,0,4:T(8,128)} %copy.383, f32[96,3,5,2,192]{0,2,3,1,4:T(8,128)} %copy.382, f32[96,3,5,2,192]{0,2,3,1,4:T(8,128)} %copy.379, f32[192,3,5,2,96]{4,3,2,1,0:T(2,128)S(1)} %copy-done.8, f32[192,3,5,2,96]{4,2,3,1,0:T(8,128)} %gather_fusion.9, ...), kind=kLoop, calls=%fused_computation.95 | loop fusion | flops 6635520 | bytes 13400928 | tf_op jit(solution)/shard_map/add | solution.py:177
  653.1 25.2 %fusion.5 = f32[3,5,2,96,192]{3,1,2,0,4:T(8,128)} fusion(f32[3,5,2,96,192]{3,1,2,0,4:T(8,128)S(1)} %bitcast.173, f32[3,5,4,98,194]{3,1,2,0,4:T(8,128)} %select_maximum_fusion, f32[3,5,2,98,1]{3,1,2,0,4:T(8,128)S(1)} %collective-permute-done.23, f32[3,5,2,1,192]{3,1,2,0,4:T(8,128)} %copy.385, f32[3,5,2,1,192]{3,1,2,0,4:T(8,128)} %copy.387, ...), kind=kLoop, calls=%fused_computation.52 | loop fusion | flops 11612160 | bytes 8990728 | tf_op jit(solution)/shard_map/add | solution.py:181
  (422 shorter events, 346.3 us)
Async XLA Ops:
  7.2 18.0 %copy-start.12 = (f32[5,2,64,128]{3,2,1,0:T(8,128)S(1)}, f32[5,2,64,128]{3,2,1,0:T(8,128)}, u32[]{:S(2)}) copy-start(f32[5,2,64,128]{3,2,1,0:T(8,128)} %param.18) | copy-start | bytes 983044
  7.2 18.0 %copy-start.21 = (f32[5]{0:T(128)S(1)}, f32[5]{0:T(128)}, u32[]{:S(2)}) copy-start(f32[5]{0:T(128)} %param.21) | copy-start | bytes 64
  7.2 18.0 %copy-start.22 = (f32[5]{0:T(128)S(1)}, f32[5]{0:T(128)}, u32[]{:S(2)}) copy-start(f32[5]{0:T(128)} %param.20) | copy-start | bytes 64
  7.2 224.4 %all-gather.5.cloned.1.call-start = ((), (), s32[]{:S(2)}) async-start(), calls=%async_computation | async-start | bytes 4177920 | tf_op jit(solution)/shard_map/all_gather | solution.py:157
  8.1 8.9 %collective-permute-start = (f32[5,2,1,128]{3,2,1,0:T(1,128)S(1)}, f32[5,2,1,128]{3,2,1,0:T(1,128)S(1)}, u32[]{:S(2)}, u32[]{:S(2)}) collective-permute-start(f32[5,2,1,128]{3,2,1,0:T(1,128)S(1)} %get-tuple-element.436), channel_id=1, source_target_pairs={{4,0},{8,4},{12,8},{5,1},{9,5},{13,9},{6,2},{10,6},{14,10},{7,3},{... | collective-permute-start | bytes 15368 | tf_op jit(solution)/shard_map/ppermute | solution.py:21
  9.4 7.6 %collective-permute-start.1 = (f32[5,2,1,128]{3,2,1,0:T(1,128)S(1)}, f32[5,2,1,128]{3,2,1,0:T(1,128)S(1)}, u32[]{:S(2)}, u32[]{:S(2)}) collective-permute-start(f32[5,2,1,128]{3,2,1,0:T(1,128)S(1)} %get-tuple-element.435), channel_id=1, source_target_pairs={{0,4},{4,8},{8,12},{1,5},{5,9},{9,13},{2,6},{6,10},{10,14},{3,7},{... | collective-permute-start | bytes 15368 | tf_op jit(solution)/shard_map/ppermute | solution.py:19
  18.2 4.4 collective-permute-start.2
  19.5 4.3 collective-permute-start.3
  80.1 154.9 %all-gather.7.cloned.1.call-start = ((), (), s32[]{:S(2)}) async-start(), calls=%async_computation.1 | async-start | bytes 4177920 | tf_op jit(solution)/shard_map/all_gather | solution.py:157
  80.2 7.1 %collective-permute-start.4 = (f32[5,2,1,128]{3,2,1,0:T(1,128)S(1)}, f32[5,2,1,128]{3,2,1,0:T(1,128)S(1)}, u32[]{:S(2)}, u32[]{:S(2)}) collective-permute-start(f32[5,2,1,128]{3,2,1,0:T(1,128)S(1)} %get-tuple-element.434), channel_id=1, source_target_pairs={{4,0},{8,4},{12,8},{5,1},{9,5},{13,9},{6,2},{10,6},{14,10},{7,3},{... | collective-permute-start | bytes 15368 | tf_op jit(solution)/shard_map/ppermute | solution.py:21
  81.5 6.8 collective-permute-start.5
  88.5 7.4 %collective-permute-start.6 = (f32[5,2,66,1]{3,2,1,0:T(8,128)S(1)}, f32[5,2,66,1]{3,2,1,0:T(8,128)S(1)}, u32[]{:S(2)}, u32[]{:S(2)}) collective-permute-start(f32[5,2,66,1]{3,2,1,0:T(8,128)S(1)} %get-tuple-element.430), channel_id=1, source_target_pairs={{1,0},{2,1},{3,2},{5,4},{6,5},{7,6},{9,8},{10,9},{11,10},{13,12},{... | collective-permute-start | bytes 7928 | tf_op jit(solution)/shard_map/ppermute | solution.py:21
  89.8 7.3 %collective-permute-start.7 = (f32[5,2,66,1]{3,2,1,0:T(8,128)S(1)}, f32[5,2,66,1]{3,2,1,0:T(8,128)S(1)}, u32[]{:S(2)}, u32[]{:S(2)}) collective-permute-start(f32[5,2,66,1]{3,2,1,0:T(8,128)S(1)} %get-tuple-element.429), channel_id=1, source_target_pairs={{0,1},{1,2},{2,3},{4,5},{5,6},{6,7},{8,9},{9,10},{10,11},{12,13},{... | collective-permute-start | bytes 7928 | tf_op jit(solution)/shard_map/ppermute | solution.py:19
  101.6 58.6 %copy-start.44 = (s32[6]{0:T(128)S(1)}, s32[6]{0:T(128)}, u32[]{:S(2)}) copy-start(s32[6]{0:T(128)} %param.23) | copy-start | bytes 76
  153.5 18.9 %collective-permute-start.9 = (f32[3,5,2,6,192]{4,2,3,1,0:T(2,128)S(1)}, f32[3,5,2,6,192]{4,2,3,1,0:T(2,128)S(1)}, u32[]{:S(2)}, u32[]{:S(2)}) collective-permute-start(f32[3,5,2,6,192]{4,2,3,1,0:T(2,128)S(1)} %copy.393), channel_id=1, source_target_pairs={{4,0},{8,4},{12,8},{5,1},{9,5},{13,9},{6,2},{10,6},{14,10},{7,3},{... | collective-permute-start | bytes 414728 | tf_op jit(solution)/shard_map/ppermute | solution.py:21
  154.9 20.8 %collective-permute-start.8 = (f32[3,5,2,6,192]{4,2,3,1,0:T(2,128)S(1)}, f32[3,5,2,6,192]{4,2,3,1,0:T(2,128)}, u32[]{:S(2)}, u32[]{:S(2)}) collective-permute-start(f32[3,5,2,6,192]{4,2,3,1,0:T(2,128)S(1)} %copy.392), channel_id=1, source_target_pairs={{0,4},{4,8},{8,12},{1,5},{5,9},{9,13},{2,6},{6,10},{10,14},{3,7},{... | collective-permute-start | bytes 414728 | tf_op jit(solution)/shard_map/ppermute | solution.py:19
  181.5 12.1 %collective-permute-start.11 = (f32[3,5,2,108,6]{3,2,4,1,0:T(2,128)S(1)}, f32[3,5,2,108,6]{3,2,4,1,0:T(2,128)S(1)}, u32[]{:S(2)}, u32[]{:S(2)}) collective-permute-start(f32[3,5,2,108,6]{3,2,4,1,0:T(2,128)S(1)} %get-tuple-element.420), channel_id=1, source_target_pairs={{1,0},{3,2},{5,4},{7,6},{9,8},{11,10},{13,12},{15,14},{17,16},{19,... | collective-permute-start | bytes 233288 | tf_op jit(solution)/shard_map/ppermute | solution.py:21
  182.9 10.9 %collective-permute-start.10 = (f32[3,5,2,108,6]{3,2,4,1,0:T(2,128)S(1)}, f32[3,5,2,108,6]{3,2,4,1,0:T(2,128)S(1)}, u32[]{:S(2)}, u32[]{:S(2)}) collective-permute-start(f32[3,5,2,108,6]{3,2,4,1,0:T(2,128)S(1)} %get-tuple-element.419), channel_id=1, source_target_pairs={{0,1},{2,3},{4,5},{6,7},{8,9},{10,11},{12,13},{14,15},{16,17},{18,... | collective-permute-start | bytes 233288 | tf_op jit(solution)/shard_map/ppermute | solution.py:19
  239.0 23.5 %copy-start.43 = (pred[192]{0:T(512)(128)(4,1)S(1)}, pred[192]{0:T(512)(128)(4,1)}, u32[]{:S(2)}) copy-start(pred[192]{0:T(512)(128)(4,1)} %get-tuple-element.488) | copy-start | bytes 580
  294.0 22.7 %copy-start.42 = (pred[192]{0:T(512)(128)(4,1)S(1)}, pred[192]{0:T(512)(128)(4,1)}, u32[]{:S(2)}) copy-start(pred[192]{0:T(512)(128)(4,1)} %get-tuple-element.489) | copy-start | bytes 580
  410.7 9.7 %collective-permute-start.12 = (f32[3,5,2,1,192]{4,2,3,1,0:T(2,128)S(1)}, f32[3,5,2,1,192]{4,2,3,1,0:T(2,128)S(1)}, u32[]{:S(2)}, u32[]{:S(2)}) collective-permute-start(f32[3,5,2,1,192]{4,2,3,1,0:T(2,128)S(1)} %copy.358), channel_id=1, source_target_pairs={{4,0},{8,4},{12,8},{5,1},{9,5},{13,9},{6,2},{10,6},{14,10},{7,3},{... | collective-permute-start | bytes 69128 | tf_op jit(solution)/shard_map/ppermute | solution.py:21
  415.8 8.4 %collective-permute-start.13 = (f32[3,5,2,1,192]{4,2,3,1,0:T(2,128)S(1)}, f32[3,5,2,1,192]{4,2,3,1,0:T(2,128)S(1)}, u32[]{:S(2)}, u32[]{:S(2)}) collective-permute-start(f32[3,5,2,1,192]{4,2,3,1,0:T(2,128)S(1)} %copy.360), channel_id=1, source_target_pairs={{0,4},{4,8},{8,12},{1,5},{5,9},{9,13},{2,6},{6,10},{10,14},{3,7},{... | collective-permute-start | bytes 69128 | tf_op jit(solution)/shard_map/ppermute | solution.py:19
  429.1 4.9 collective-permute-start.14
  430.7 4.0 collective-permute-start.15
  478.0 9.9 %collective-permute-start.17 = (f32[3,5,2,6,192]{4,2,3,1,0:T(2,128)S(1)}, f32[3,5,2,6,192]{4,2,3,1,0:T(2,128)S(1)}, u32[]{:S(2)}, u32[]{:S(2)}) collective-permute-start(f32[3,5,2,6,192]{4,2,3,1,0:T(2,128)S(1)} %copy.365), channel_id=1, source_target_pairs={{4,0},{8,4},{12,8},{5,1},{9,5},{13,9},{6,2},{10,6},{14,10},{7,3},{... | collective-permute-start | bytes 414728 | tf_op jit(solution)/shard_map/ppermute | solution.py:21
  483.2 8.7 %collective-permute-start.16 = (f32[3,5,2,6,192]{4,2,3,1,0:T(2,128)S(1)}, f32[3,5,2,6,192]{4,2,3,1,0:T(2,128)S(1)}, u32[]{:S(2)}, u32[]{:S(2)}) collective-permute-start(f32[3,5,2,6,192]{4,2,3,1,0:T(2,128)S(1)} %copy.364), channel_id=1, source_target_pairs={{0,4},{4,8},{8,12},{1,5},{5,9},{9,13},{2,6},{6,10},{10,14},{3,7},{... | collective-permute-start | bytes 414728 | tf_op jit(solution)/shard_map/ppermute | solution.py:19
  497.9 73.8 %collective-permute-start.19 = (f32[3,5,2,108,6]{3,1,2,0,4:T(8,128)}, f32[3,5,2,108,6]{3,1,2,0,4:T(8,128)S(1)}, u32[]{:S(2)}, u32[]{:S(2)}) collective-permute-start(f32[3,5,2,108,6]{3,1,2,0,4:T(8,128)} %get-tuple-element.416), channel_id=1, source_target_pairs={{1,0},{3,2},{5,4},{7,6},{9,8},{11,10},{13,12},{15,14},{17,16},{19,... | collective-permute-start | bytes 233288 | tf_op jit(solution)/shard_map/ppermute | solution.py:21
  499.2 72.5 %collective-permute-start.18 = (f32[3,5,2,108,6]{3,1,2,0,4:T(8,128)S(1)}, f32[3,5,2,108,6]{3,1,2,0,4:T(8,128)}, u32[]{:S(2)}, u32[]{:S(2)}) collective-permute-start(f32[3,5,2,108,6]{3,1,2,0,4:T(8,128)S(1)} %get-tuple-element.415), channel_id=1, source_target_pairs={{0,1},{2,3},{4,5},{6,7},{8,9},{10,11},{12,13},{14,15},{16,17},{18,... | collective-permute-start | bytes 233288 | tf_op jit(solution)/shard_map/ppermute | solution.py:19
  622.5 10.3 %collective-permute-start.20 = (f32[3,5,2,1,192]{4,2,3,1,0:T(2,128)S(1)}, f32[3,5,2,1,192]{4,2,3,1,0:T(2,128)S(1)}, u32[]{:S(2)}, u32[]{:S(2)}) collective-permute-start(f32[3,5,2,1,192]{4,2,3,1,0:T(2,128)S(1)} %copy.384), channel_id=1, source_target_pairs={{4,0},{8,4},{12,8},{5,1},{9,5},{13,9},{6,2},{10,6},{14,10},{7,3},{... | collective-permute-start | bytes 69128 | tf_op jit(solution)/shard_map/ppermute | solution.py:21
  627.8 8.9 %collective-permute-start.21 = (f32[3,5,2,1,192]{4,2,3,1,0:T(2,128)S(1)}, f32[3,5,2,1,192]{4,2,3,1,0:T(2,128)S(1)}, u32[]{:S(2)}, u32[]{:S(2)}) collective-permute-start(f32[3,5,2,1,192]{4,2,3,1,0:T(2,128)S(1)} %copy.386), channel_id=1, source_target_pairs={{0,4},{4,8},{8,12},{1,5},{5,9},{9,13},{2,6},{6,10},{10,14},{3,7},{... | collective-permute-start | bytes 69128 | tf_op jit(solution)/shard_map/ppermute | solution.py:19
  641.7 4.7 collective-permute-start.22
  643.3 4.0 collective-permute-start.23
  (44 other events, 392.4 us)
Sparse Core Ops, SparseCore 0:
  80.3 57.8 all-gather.4
  152.4 59.8 all-gather.6
